TPU v7x, 32 devices: a whole 2x2x4 slice. The times are simulated.
32 devices in a mesh: groups: 2 (over y), tm: 4 (over z), head: 2 (over x), mp: 2 (over core).
Axes of the slice: x: 2, y: 2, z: 4, core: 2. Of those that a mesh axis runs over, the one named last changes fastest.
Arguments:
- queries: bfloat16 [2048, 2048], P(('groups', 'tm'), ('head', 'mp')), parts along dimension 0, may hold values from -6 to 6
- key_rows: bfloat16 [2048, 2048], P(('groups', 'tm'), ('head', 'mp')), parts along dimension 0, may hold values from -6 to 6
- value_rows: bfloat16 [2048, 2048], P(('groups', 'tm'), ('head', 'mp')), parts along dimension 0, may hold values from -12 to 12
- cotangent: bfloat16 [2048, 2048], P(('groups', 'tm'), ('head', 'mp')), parts along dimension 0, may hold values from -12 to 12
- block_active: int32 [16], P('groups'), parts along dimension 0, may hold values from 0 to 1
- send_counts: int32 [8, 2], P('groups'), parts along dimension 0, may hold values from 0 to 1, as said below
- block_mask: int32 [16, 8], P('groups'), parts along dimension 0, may hold values from 0 to 1, as said below
Outputs:
- attended: bfloat16 [4096, 2048], P(('groups', 'tm'), ('head', 'mp')), parts along dimension 0
- query_grad: bfloat16 [4096, 2048], P(('groups', 'tm'), ('head', 'mp')), parts along dimension 0
- key_grad: bfloat16 [2048, 2048], P(('groups', 'tm'), ('head', 'mp')), parts along dimension 0
- value_grad: bfloat16 [2048, 2048], P(('groups', 'tm'), ('head', 'mp')), parts along dimension 0
There are 2 independent parts, one for each index of `groups`. A program takes and returns all parts, laid end to end along the dimension named above; each array names one. Nothing has to cross between parts.
Inputs may be any that keep to these rules, and one draw needn't show every extreme that they name: `send_counts`: column 0 of row i counts the first blocks of shard i that go to shard i-1, column 1 its last blocks that go to shard i+1 (shard 0 follows shard 4-1); the two sum to at most 2; every block that is handed on is active. `block_mask`: the diagonal is 1.
All inputs are finite; a program needn't handle non-finite values.
Results may differ from a plain program's by a relative error of at most 0.02.
Values may be sent and summed in bfloat16 or wider, within the bound.
A program may use at most 64 MiB of HBM per device.

v0:
```python
import math

import jax
import jax.numpy as jnp
from jax import lax
from jax.sharding import PartitionSpec as P

HD = 128
BLK = 128
CAP = 1


very_low = -1e30


def extended_2(shard, sides, width):
    for axis, dim in sides:
        peers, length = (lax.axis_size(axis), shard.shape[dim])
        up = [(i, (i + 1) % peers) for i in range(peers)]
        down = [(j, i) for i, j in up]
        last = lax.slice_in_dim(shard, length - width, length, axis=dim)
        first = lax.slice_in_dim(shard, 0, width, axis=dim)
        before = lax.ppermute(last, axis, up)
        after = lax.ppermute(first, axis, down)
        shard = jnp.concatenate([before, shard, after], axis=dim)
    return shard


def pick(table, positions, extent):
    matches = positions[:, None] == jnp.arange(extent, dtype=jnp.int32)[None, :]
    return jnp.sum(jnp.where(matches, table[None, :], 0), axis=1)


def slot_layout(block_active, send_counts, block_mask, shards, own_blocks, capacity):
    slot_count = own_blocks + 2 * capacity
    all_blocks = shards * own_blocks
    places = jnp.arange(shards * slot_count, dtype=jnp.int32)
    device = places // slot_count
    slot_index = places % slot_count
    before = (device + shards - 1) % shards
    following = (device + 1) % shards
    to_left = send_counts[:, 0]
    to_right = send_counts[:, 1]
    from_before = slot_index < capacity
    from_after = slot_index >= capacity + own_blocks
    owner_shard = jnp.where(from_before, before, jnp.where(from_after, following, device))
    local_block = jnp.where(
        from_before,
        own_blocks - capacity + slot_index,
        jnp.where(from_after, slot_index - capacity - own_blocks, slot_index - capacity),
    )
    middle_ok = (local_block >= pick(to_left, device, shards)) & (
        local_block < own_blocks - pick(to_right, device, shards)
    )
    holds_record = jnp.where(
        from_before,
        slot_index >= capacity - pick(to_right, before, shards),
        jnp.where(from_after, local_block < pick(to_left, following, shards), middle_ok),
    )
    anchor = owner_shard * own_blocks + local_block
    onehot = (anchor[:, None] == jnp.arange(all_blocks, dtype=jnp.int32)[None, :]).astype(
        jnp.float32
    )
    seeing = (block_mask * block_active[None, :]).astype(jnp.float32)
    block_rows = jnp.dot(onehot, seeing, precision=lax.Precision.HIGHEST)
    active = jnp.dot(onehot, block_active.astype(jnp.float32), precision=lax.Precision.HIGHEST)
    present = jnp.where(holds_record, active, 0.0)
    return (anchor, block_rows * present[:, None], present)


def block_hot(offset, length, extent):
    blocks = (offset + jnp.arange(length, dtype=jnp.int32)) // BLK
    return (blocks[:, None] == jnp.arange(extent, dtype=jnp.int32)[None, :]).astype(jnp.bfloat16)


def sweep(update, running, pieces, offset):
    row_count = pieces[0].shape[0]
    step_rows = math.gcd(row_count, 1024)
    if step_rows == row_count:
        return update(running, pieces, offset)

    def one_turn(turn_index, carried):
        part_pieces = tuple(
            (
                lax.dynamic_slice_in_dim(member, turn_index * step_rows, step_rows, 0)
                for member in pieces
            )
        )
        return update(carried, part_pieces, offset + turn_index * step_rows)

    return lax.fori_loop(0, row_count // step_rows, one_turn, running)


def body(queries, key_rows, value_rows, cotangent, block_active, send_counts, block_mask):
    shards = lax.axis_size("tm")
    shard_index = lax.axis_index("tm")
    model_width = queries.shape[1]
    head_count = model_width // HD
    own_rows = queries.shape[0]
    own_blocks = own_rows // BLK
    all_blocks = block_active.shape[0]
    slot_count = own_blocks + 2 * CAP
    slot_rows = slot_count * BLK
    scaling = 1.0 / math.sqrt(HD)
    anchor, table, present = slot_layout(
        block_active, send_counts, block_mask, shards, own_blocks, CAP
    )
    records = jnp.concatenate([queries, cotangent], axis=1)
    extended = extended_2(records, (("tm", 0),), CAP * BLK)
    query_slots = extended[:, :model_width].reshape(slot_rows, head_count, HD)
    cotan_slots = extended[:, model_width:].reshape(slot_rows, head_count, HD)
    my_table = lax.dynamic_slice_in_dim(table, shard_index * slot_count, slot_count, 0)
    query_table = jnp.repeat(my_table, BLK, axis=0).astype(jnp.bfloat16)
    live = (
        jnp.repeat(lax.dynamic_slice_in_dim(present, shard_index * slot_count, slot_count, 0), BLK)
        > 0.5
    )
    keys_all, values_all = (
        lax.all_gather(key_rows, "tm", axis=0, tiled=True),
        lax.all_gather(value_rows, "tm", axis=0, tiled=True),
    )

    def own_scores(key_piece, offset):
        allowed = (
            lax.dot_general(
                query_table,
                block_hot(offset, key_piece.shape[0], all_blocks),
                (((1,), (1,)), ((), ())),
                preferred_element_type=jnp.float32,
            )[:, None, :]
            > 0.5
        )
        scores = (
            jnp.einsum("qhd,khd->qhk", query_slots, key_piece, preferred_element_type=jnp.float32)
            * scaling
        )
        return (allowed, scores)

    def forward(running, pieces, offset):
        peak, masses, accum = running
        key_piece = pieces[0].reshape(-1, head_count, HD)
        value_piece = pieces[1].reshape(-1, head_count, HD)
        allowed, scores = own_scores(key_piece, offset)
        new_peak = jnp.maximum(peak, jnp.max(jnp.where(allowed, scores, very_low), axis=2))
        weights = jnp.where(
            allowed, jnp.exp(jnp.where(allowed, scores - new_peak[:, :, None], 0.0)), 0.0
        )
        shrink = jnp.exp(peak - new_peak)
        masses = masses * shrink + jnp.sum(weights, axis=2)
        accum = accum * shrink[:, :, None] + jnp.einsum(
            "qhk,khd->qhd",
            weights.astype(jnp.bfloat16),
            value_piece,
            preferred_element_type=jnp.float32,
        )
        return (new_peak, masses, accum)

    initial = (
        jnp.full((slot_rows, head_count), very_low, jnp.float32),
        jnp.zeros((slot_rows, head_count), jnp.float32),
        jnp.zeros((slot_rows, head_count, HD), jnp.float32),
    )
    peak, masses, accum = sweep(forward, initial, (keys_all, values_all), 0)
    denominator = jnp.where(live[:, None], masses, 1.0)
    attended = (accum / denominator[:, :, None]).astype(jnp.bfloat16)
    log_norm = peak + jnp.log(denominator)
    deltas = jnp.sum(cotan_slots.astype(jnp.float32) * attended.astype(jnp.float32), axis=2)

    def own_gradients(key_piece, value_piece, offset):
        allowed, scores = own_scores(key_piece, offset)
        probs = jnp.where(
            allowed, jnp.exp(jnp.where(allowed, scores - log_norm[:, :, None], 0.0)), 0.0
        )
        weight_grad = jnp.einsum(
            "qhd,khd->qhk", cotan_slots, value_piece, preferred_element_type=jnp.float32
        )
        return (probs, (probs * (weight_grad - deltas[:, :, None])).astype(jnp.bfloat16))

    zero_query = jnp.zeros((slot_rows, head_count, HD), jnp.float32)

    def query_pass(query_sum, pieces, offset):
        key_piece = pieces[0].reshape(-1, head_count, HD)
        value_piece = pieces[1].reshape(-1, head_count, HD)
        probs, score_grad = own_gradients(key_piece, value_piece, offset)
        return query_sum + jnp.einsum(
            "qhk,khd->qhd", score_grad, key_piece, preferred_element_type=jnp.float32
        )

    query_sum = sweep(query_pass, zero_query, (keys_all, values_all), 0)
    own_keys = key_rows.reshape(own_rows, head_count, HD)
    own_values = value_rows.reshape(own_rows, head_count, HD)
    own_hot = block_hot(shard_index * own_rows, own_rows, all_blocks)
    slot_table = table.astype(jnp.bfloat16)
    logsum_all, delta_all = (
        lax.all_gather(log_norm, "tm", axis=0, tiled=True),
        lax.all_gather(deltas, "tm", axis=0, tiled=True),
    )

    def owner_work(running, pieces, offset):
        key_sum, value_sum = running
        query_piece, cotan_piece = pieces
        row_count = query_piece.shape[0]
        logsum_piece = lax.dynamic_slice_in_dim(logsum_all, offset, row_count, 0)
        delta_piece = lax.dynamic_slice_in_dim(delta_all, offset, row_count, 0)
        piece_table = jnp.dot(
            block_hot(offset, row_count, shards * slot_count),
            slot_table,
            preferred_element_type=jnp.float32,
        ).astype(jnp.bfloat16)
        allowed = (
            lax.dot_general(
                piece_table, own_hot, (((1,), (1,)), ((), ())), preferred_element_type=jnp.float32
            )[:, None, :]
            > 0.5
        )
        query_three = query_piece.reshape(row_count, head_count, HD)
        cotan_three = cotan_piece.reshape(row_count, head_count, HD)
        scores = (
            jnp.einsum("qhd,khd->qhk", query_three, own_keys, preferred_element_type=jnp.float32)
            * scaling
        )
        probs = jnp.where(
            allowed, jnp.exp(jnp.where(allowed, scores - logsum_piece[:, :, None], 0.0)), 0.0
        )
        weight_grad = jnp.einsum(
            "qhd,khd->qhk", cotan_three, own_values, preferred_element_type=jnp.float32
        )
        score_grad = (probs * (weight_grad - delta_piece[:, :, None])).astype(jnp.bfloat16)
        key_sum = key_sum + jnp.einsum(
            "qhk,qhd->khd", score_grad, query_three, preferred_element_type=jnp.float32
        )
        value_sum = value_sum + jnp.einsum(
            "qhk,qhd->khd",
            probs.astype(jnp.bfloat16),
            cotan_three,
            preferred_element_type=jnp.float32,
        )
        return (key_sum, value_sum)

    key_zero = jnp.zeros((own_rows, head_count, HD), jnp.float32)
    key_sum, value_sum = sweep(
        owner_work,
        (key_zero, key_zero),
        (
            lax.all_gather(query_slots.reshape(slot_rows, model_width), "tm", axis=0, tiled=True),
            lax.all_gather(cotan_slots.reshape(slot_rows, model_width), "tm", axis=0, tiled=True),
        ),
        jnp.int32(0),
    )
    key_grad = (key_sum * scaling).astype(jnp.bfloat16).reshape(own_rows, model_width)
    value_grad = value_sum.astype(jnp.bfloat16).reshape(own_rows, model_width)
    query_grad = (query_sum * scaling).astype(jnp.bfloat16).reshape(slot_rows, model_width)
    return (attended.reshape(slot_rows, model_width), query_grad, key_grad, value_grad)


def solution(mesh):
    in_specs = (
        P(("groups", "tm"), ("head", "mp")),
        P(("groups", "tm"), ("head", "mp")),
        P(("groups", "tm"), ("head", "mp")),
        P(("groups", "tm"), ("head", "mp")),
        P("groups"),
        P("groups", None),
        P("groups", None),
    )
    out_specs = (
        P(("groups", "tm"), ("head", "mp")),
        P(("groups", "tm"), ("head", "mp")),
        P(("groups", "tm"), ("head", "mp")),
        P(("groups", "tm"), ("head", "mp")),
    )
    return jax.shard_map(body, mesh=mesh, in_specs=in_specs, out_specs=out_specs, check_vma=False)
```

profile of v0, /device:TPU:0, one launch (start us, length us, event | category | flops | bytes accessed | tf_op | source)
XLA Modules:
  0.0 210.3 jit_solution(11697124278992950127)
XLA Ops:
  7.3 1.8 copy.78
  9.2 0.7 all-gather.7.cloned.1.call-update
  9.9 1.1 copy.76
  11.0 1.1 copy.77
  12.1 5.1 %collective-permute-start.1 = (bf16[128,1024]{0,1:T(8,128)(2,1)S(1)}, bf16[128,1024]{0,1:T(8,128)(2,1)S(1)}, u32[]{:S(2)}, u32[]{:S(2)}) collective-permute-start(bf16[128,1024]{0,1:T(8,128)(2,1)S(1)} %get-tuple-element.421), channel_id=1, source_target_pairs={{4,0},{8,4},{12,8},{0,12},{5,1},{9,5},{13,9},{1,13},{6,2},{10,6},{... | collective-permute-start | bytes 786440 | tf_op jit(solution)/shard_map/ppermute | solution.py:24
  17.2 9.6 %collective-permute-done.1 = bf16[128,1024]{0,1:T(8,128)(2,1)S(1)} collective-permute-done((bf16[128,1024]{0,1:T(8,128)(2,1)S(1)}, bf16[128,1024]{0,1:T(8,128)(2,1)S(1)}, u32[]{:S(2)}, u32[]{:S(2)}) %collective-permute-start.1) | collective-permute-done | bytes 262176 | tf_op jit(solution)/shard_map/ppermute | solution.py:24
  26.8 10.1 %collective-permute-done = bf16[128,1024]{0,1:T(8,128)(2,1)S(1)} collective-permute-done((bf16[128,1024]{0,1:T(8,128)(2,1)S(1)}, bf16[128,1024]{0,1:T(8,128)(2,1)S(1)}, u32[]{:S(2)}, u32[]{:S(2)}) %collective-permute-start) | collective-permute-done | bytes 262176 | tf_op jit(solution)/shard_map/ppermute | solution.py:23
  37.0 0.1 pad_maximum_fusion
  37.1 1.1 fusion.82
  38.3 0.1 copy.85
  38.5 0.1 select_reduce_fusion.3
  38.6 0.2 fusion.63
  38.8 0.2 convolution_multiply_fusion
  38.9 0.1 copy.86
  39.0 0.2 copy.87
  39.2 0.8 copy.88
  40.1 0.1 dynamic-slice_compare_fusion
  40.3 0.6 convolution_compare_fusion.1
  40.9 7.4 %all-gather.5.cloned.1.call-done = bf16[1024,512]{0,1:T(8,128)(2,1)} async-done(((bf16[256,512]{0,1:T(8,128)(2,1)}), bf16[1024,512]{0,1:T(8,128)(2,1)}) %all-gather.5.cloned.1.call-update) | async-done | bytes 1048592 | tf_op jit(solution)/shard_map/all_gather | solution.py:119
  48.3 6.2 %fusion.34 = (f32[512,4]{0,1:T(4,128)S(1)}, f32[4,512,1024]{2,1,0:T(8,128)}) fusion(pred[512,1024]{1,0:T(8,128)(4,1)S(1)} %convolution_compare_fusion.1, bf16[512,4,128]{0,2,1:T(8,128)(2,1)S(1)} %bitcast.173, bf16[1024,4,128]{0,2,1:T(8,128)(2,1)} %bitcast.176), kind=kOutput, calls=%fused_computation.46 | convolution fusion | flops 543160320 | bytes 10493952 | tf_op jit(solution)/shard_map/qhd,khd->qhk/dot_general | solution.py:134
  54.5 22.5 %all-gather.7.cloned.1.call-done = bf16[1024,512]{1,0:T(8,128)(2,1)} async-done(((bf16[256,512]{1,0:T(8,128)(2,1)}), bf16[1024,512]{1,0:T(8,128)(2,1)}) %all-gather.7.cloned.1.call-update) | async-done | bytes 1048592 | tf_op jit(solution)/shard_map/all_gather | solution.py:120
  77.1 2.3 %copy.81 = bf16[1024,512]{0,1:T(8,128)(2,1)} copy(bf16[1024,512]{1,0:T(8,128)(2,1)} %all-gather.7.cloned.1.call-done) | data formatting | bytes 2097152 | tf_op jit(solution)/shard_map/all_gather | solution.py:120
  79.4 5.3 %fusion.41 = f32[512,4]{0,1:T(4,128)S(1)} fusion(f32[4,512,1024]{2,1,0:T(8,128)} %get-tuple-element.426, f32[512,4]{0,1:T(4,128)S(1)} %broadcast_maximum_fusion, pred[512,1024]{1,0:T(8,128)(4,1)S(1)} %convolution_compare_fusion.1), kind=kLoop, calls=%fused_computation.53 | loop fusion | flops 10483712 | bytes 8929280 | tf_op jit(solution)/shard_map/reduce_sum | solution.py:149
  84.7 0.6 copy-done
  85.3 5.0 %multiply_reduce_fusion = (f32[512,4]{0,1:T(4,128)S(1)}, bf16[512,4,128]{0,2,1:T(8,128)(2,1)}) fusion(bf16[512,1024]{0,1:T(8,128)(2,1)S(1)} %pad_maximum_fusion, f32[512,4]{0,1:T(4,128)S(1)} %get-tuple-element.413, bf16[1024,4,128]{0,2,1:T(8,128)(2,1)} %bitcast.180, f32[4,512,1024]{2,1,0:T(8,128)S(1)} %copy-done, f32[512,4]{0,1:T(4,128)S(1)} %broadcast_maximum_fusion, ...), kind=kOutput, calls=%fused_computation.69 | convolution fusion | flops 549189632 | bytes 11042816 | tf_op jit(solution)/shard_map/qhk,khd->qhd/dot_general | solution.py:150
  90.3 2.0 copy.91
  92.4 8.0 %fusion.60 = bf16[4,512,128]{1,2,0:T(8,128)(2,1)S(1)} fusion(bf16[1024,4,128]{0,2,1:T(8,128)(2,1)S(1)} %bitcast.177, f32[4,512,1024]{2,1,0:T(8,128)} %get-tuple-element.426, f32[512,4]{0,1:T(4,128)S(1)} %get-tuple-element.427, f32[512,4]{0,1:T(4,128)S(1)} %get-tuple-element.412, pred[512,1024]{1,0:T(8,128)(4,1)S(1)} %convolution_compare_fusion.1, ...), kind=kOutput, calls=%fused_computation.64 | convolution fusion | flops 1088946176 | bytes 12075008 | tf_op jit(solution)/shard_map/qhk,khd->qhd/dot_general | solution.py:185
  100.4 1.0 copy.92
  101.4 13.4 %all_gather.21 = f32[2048,4]{0,1:T(4,128)S(1)} all-gather(f32[512,4]{0,1:T(4,128)S(1)} %get-tuple-element.412), channel_id=1, replica_groups=mesh['groups'=2,'tm'=4,'head'=2,'mp'=2] {'tm'}, dimensions={0}, use_global_device_ids=true | all-gather | bytes 40960 | tf_op jit(solution)/shard_map/all_gather | solution.py:195
  114.7 13.3 %all_gather.23 = f32[2048,4]{0,1:T(4,128)S(1)} all-gather(f32[512,4]{0,1:T(4,128)S(1)} %get-tuple-element.427), channel_id=1, replica_groups=mesh['groups'=2,'tm'=4,'head'=2,'mp'=2] {'tm'}, dimensions={0}, use_global_device_ids=true | all-gather | bytes 40960 | tf_op jit(solution)/shard_map/all_gather | solution.py:196
  128.0 43.1 %all-gather.11.cloned.1.call-done = bf16[2048,512]{0,1:T(8,128)(2,1)} async-done(((bf16[512,512]{0,1:T(8,128)(2,1)}), bf16[2048,512]{0,1:T(8,128)(2,1)}) %all-gather.11.cloned.1.call-update) | async-done | bytes 2097168 | tf_op jit(solution)/shard_map/all_gather | solution.py:246
  171.1 28.8 %while.18 = (s32[]{:T(128)}, f32[256,4,128]{0,2,1:T(8,128)}, f32[256,4,128]{0,2,1:T(8,128)}, bf16[2048,512]{0,1:T(8,128)(2,1)}, bf16[16,8]{0,1:T(8,128)(2,1)S(1)...) while((s32[]{:T(128)}, f32[256,4,128]{0,2,1:T(8,128)}, ...), condition=%wide.region_8.9_spmd.clone, body=%wide.region_7.8_spmd.clone.sunk | while | flops 1091612672 | bytes 32892488 | solution.py:91
  171.1 1.7 constant_dynamic-slice_fusion.6
  172.9 2.7 %fusion.119 = f32[4,1024,256]{2,1,0:T(8,128)} fusion(bf16[1024,4,128]{0,2,1:T(8,128)(2,1)S(1)} %bitcast.169, bf16[256,4,128]{2,0,1:T(8,128)(2,1)S(1)} %get-tuple-element.541), kind=kOutput, calls=%fused_computation.134.clone.1 | convolution fusion | flops 268435456 | bytes 5505024 | tf_op jit(solution)/shard_map/while/body/eval_jaxpr/qhd,khd->qhk/dot_general | solution.py:219
  175.6 1.3 convolution_compare_fusion.3
  176.9 4.5 %fusion.120 = f32[256,4,128]{0,2,1:T(8,128)S(1)} fusion(bf16[1024,4,128]{0,2,1:T(8,128)(2,1)S(1)} %bitcast.170, f32[4,1024,256]{2,1,0:T(8,128)} %fusion.119, bf16[1024,4,128]{0,2,1:T(8,128)(2,1)S(1)} %bitcast.171, bf16[256,4,128]{2,0,1:T(8,128)(2,1)} %get-tuple-element.544, f32[1024,4]{0,1:T(4,128)S(1)} %get-tuple-element.504, ...), kind=kOutput, calls=%fused_computation.16.clone.1 | convolution fusion | flops 544473088 | bytes 7897089 | tf_op jit(solution)/shard_map/while/body/eval_jaxpr/qhk,qhd->khd/dot_general | solution.py:229
  181.5 3.2 %fusion.121 = f32[256,4,128]{0,2,1:T(8,128)S(1)} fusion(bf16[1024,4,128]{0,2,1:T(8,128)(2,1)S(1)} %bitcast.172, f32[4,1024,256]{2,1,0:T(8,128)} %fusion.119, f32[1024,4]{0,1:T(4,128)S(1)} %get-tuple-element.505, pred[1024,256]{1,0:T(8,128)(4,1)} %convolution_compare_fusion.3, f32[256,4,128]{0,2,1:T(8,128)S(1)} %copy-done.8, pred[]{:T(512)S(6)} %compare.53), kind=kOutput, calls=%fused_computation.15.clone.1 | convolution fusion | flops 273940480 | bytes 6569985 | tf_op jit(solution)/shard_map/while/body/eval_jaxpr/qhk,qhd->khd/dot_general | solution.py:232
  184.7 0.8 copy-done.9
  185.5 1.7 constant_dynamic-slice_fusion.6
  187.3 2.7 %fusion.119 = f32[4,1024,256]{2,1,0:T(8,128)} fusion(bf16[1024,4,128]{0,2,1:T(8,128)(2,1)S(1)} %bitcast.169, bf16[256,4,128]{2,0,1:T(8,128)(2,1)S(1)} %get-tuple-element.541), kind=kOutput, calls=%fused_computation.134.clone.1 | convolution fusion | flops 268435456 | bytes 5505024 | tf_op jit(solution)/shard_map/while/body/eval_jaxpr/qhd,khd->qhk/dot_general | solution.py:219
  190.0 1.3 convolution_compare_fusion.3
  191.3 4.5 %fusion.120 = f32[256,4,128]{0,2,1:T(8,128)S(1)} fusion(bf16[1024,4,128]{0,2,1:T(8,128)(2,1)S(1)} %bitcast.170, f32[4,1024,256]{2,1,0:T(8,128)} %fusion.119, bf16[1024,4,128]{0,2,1:T(8,128)(2,1)S(1)} %bitcast.171, bf16[256,4,128]{2,0,1:T(8,128)(2,1)} %get-tuple-element.544, f32[1024,4]{0,1:T(4,128)S(1)} %get-tuple-element.504, ...), kind=kOutput, calls=%fused_computation.16.clone.1 | convolution fusion | flops 544473088 | bytes 7897089 | tf_op jit(solution)/shard_map/while/body/eval_jaxpr/qhk,qhd->khd/dot_general | solution.py:229
  195.9 3.2 %fusion.121 = f32[256,4,128]{0,2,1:T(8,128)S(1)} fusion(bf16[1024,4,128]{0,2,1:T(8,128)(2,1)S(1)} %bitcast.172, f32[4,1024,256]{2,1,0:T(8,128)} %fusion.119, f32[1024,4]{0,1:T(4,128)S(1)} %get-tuple-element.505, pred[1024,256]{1,0:T(8,128)(4,1)} %convolution_compare_fusion.3, f32[256,4,128]{0,2,1:T(8,128)S(1)} %copy-done.8, pred[]{:T(512)S(6)} %compare.53), kind=kOutput, calls=%fused_computation.15.clone.1 | convolution fusion | flops 273940480 | bytes 6569985 | tf_op jit(solution)/shard_map/while/body/eval_jaxpr/qhk,qhd->khd/dot_general | solution.py:232
  199.1 0.8 copy-done.9
  199.9 1.1 multiply_convert_fusion
  201.0 0.8 copy.100
  201.9 1.1 convert_element_type.96
  202.9 0.8 copy.101
  (58 shorter events, 0.5 us)
Async XLA Ops:
  7.2 31.1 %copy-start.5 = (bf16[256,512]{1,0:T(8,128)(2,1)S(1)}, bf16[256,512]{1,0:T(8,128)(2,1)}, u32[]{:S(2)}) copy-start(bf16[256,512]{1,0:T(8,128)(2,1)} %param.11) | copy-start | bytes 786436
  7.2 31.3 %copy-start.10 = (s32[4,2]{0,1:T(2,128)S(1)}, s32[4,2]{0,1:T(2,128)}, u32[]{:S(2)}) copy-start(s32[4,2]{0,1:T(2,128)} %param.14) | copy-start | bytes 100
  7.2 31.4 %copy-start.12 = (s32[8]{0:T(128)S(1)}, s32[8]{0:T(128)}, u32[]{:S(2)}) copy-start(s32[8]{0:T(128)} %param.13) | copy-start | bytes 100
  7.2 31.6 %copy-start.11 = (s32[8,8]{1,0:T(8,128)S(1)}, s32[8,8]{1,0:T(8,128)}, u32[]{:S(2)}) copy-start(s32[8,8]{1,0:T(8,128)} %param.15) | copy-start | bytes 772
  7.2 41.1 %all-gather.5.cloned.1.call-start = ((), (), s32[]{:S(2)}) async-start(), calls=%async_computation | async-start | bytes 1310720 | tf_op jit(solution)/shard_map/all_gather | solution.py:119
  9.1 30.0 %copy-start.2 = (bf16[256,512]{0,1:T(8,128)(2,1)S(1)}, bf16[256,512]{0,1:T(8,128)(2,1)}, u32[]{:S(2)}) copy-start(bf16[256,512]{0,1:T(8,128)(2,1)} %copy.78) | copy-start | bytes 786436
  9.1 67.9 %all-gather.7.cloned.1.call-start = ((), (), s32[]{:S(2)}) async-start(), calls=%async_computation.1 | async-start | bytes 1310720 | tf_op jit(solution)/shard_map/all_gather | solution.py:120
  9.9 118.2 %all-gather.9.cloned.1.call-start = ((), (), s32[]{:S(2)}) async-start(), calls=%async_computation.2 | async-start | bytes 2621440 | tf_op jit(solution)/shard_map/all_gather | solution.py:245
  12.1 14.7 %collective-permute-start.1 = (bf16[128,1024]{0,1:T(8,128)(2,1)S(1)}, bf16[128,1024]{0,1:T(8,128)(2,1)S(1)}, u32[]{:S(2)}, u32[]{:S(2)}) collective-permute-start(bf16[128,1024]{0,1:T(8,128)(2,1)S(1)} %get-tuple-element.421), channel_id=1, source_target_pairs={{4,0},{8,4},{12,8},{0,12},{5,1},{9,5},{13,9},{1,13},{6,2},{10,6},{... | collective-permute-start | bytes 786440 | tf_op jit(solution)/shard_map/ppermute | solution.py:24
  17.2 19.7 %collective-permute-start = (bf16[128,1024]{0,1:T(8,128)(2,1)S(1)}, bf16[128,1024]{0,1:T(8,128)(2,1)S(1)}, u32[]{:S(2)}, u32[]{:S(2)}) collective-permute-start(bf16[128,1024]{0,1:T(8,128)(2,1)S(1)} %get-tuple-element.420), channel_id=1, source_target_pairs={{0,4},{4,8},{8,12},{12,0},{1,5},{5,9},{9,13},{13,1},{2,6},{6,10},{... | collective-permute-start | bytes 786440 | tf_op jit(solution)/shard_map/ppermute | solution.py:23
  38.1 10.1 %copy-start.1 = (bf16[512,512]{0,1:T(8,128)(2,1)S(1)}, bf16[512,512]{0,1:T(8,128)(2,1)}, u32[]{:S(2)}) copy-start(bf16[512,512]{0,1:T(8,128)(2,1)} %get-tuple-element.419) | copy-start | bytes 1572868
  38.2 133.0 %all-gather.11.cloned.1.call-start = ((), (), s32[]{:S(2)}) async-start(), calls=%async_computation.3 | async-start | bytes 2621440 | tf_op jit(solution)/shard_map/all_gather | solution.py:246
  79.4 6.0 %copy-start = (f32[4,512,1024]{2,1,0:T(8,128)S(1)}, f32[4,512,1024]{2,1,0:T(8,128)}, u32[]{:S(2)}) copy-start(f32[4,512,1024]{2,1,0:T(8,128)} %get-tuple-element.426) | copy-start | bytes 25165828
  85.3 7.1 %copy-start.3 = (bf16[512,512]{0,1:T(8,128)(2,1)S(1)}, bf16[512,512]{0,1:T(8,128)(2,1)}, u32[]{:S(2)}) copy-start(bf16[512,512]{0,1:T(8,128)(2,1)} %get-tuple-element.418) | copy-start | bytes 1572868
  85.3 7.1 %copy-start.4 = (bf16[1024,512]{0,1:T(8,128)(2,1)S(1)}, bf16[1024,512]{0,1:T(8,128)(2,1)}, u32[]{:S(2)}) copy-start(bf16[1024,512]{0,1:T(8,128)(2,1)} %all-gather.5.cloned.1.call-done) | copy-start | bytes 3145732
  172.8 4.0 %copy-start.6 = (f32[256,4,128]{0,2,1:T(8,128)S(1)}, f32[256,4,128]{0,2,1:T(8,128)}, u32[]{:S(2)}) copy-start(f32[256,4,128]{0,2,1:T(8,128)} %get-tuple-element.522) | copy-start | bytes 1572868 | tf_op jit(solution)/shard_map/while
  176.9 4.5 %copy-start.8 = (f32[256,4,128]{0,2,1:T(8,128)S(1)}, f32[256,4,128]{0,2,1:T(8,128)}, u32[]{:S(2)}) copy-start(f32[256,4,128]{0,2,1:T(8,128)} %get-tuple-element.523) | copy-start | bytes 1572868 | tf_op jit(solution)/shard_map/while
  181.4 3.3 %copy-start.7 = (f32[256,4,128]{0,2,1:T(8,128)}, f32[256,4,128]{0,2,1:T(8,128)S(1)}, u32[]{:S(2)}) copy-start(f32[256,4,128]{0,2,1:T(8,128)S(1)} %fusion.120) | copy-start | bytes 1572868 | tf_op jit(solution)/shard_map/while
  184.7 0.8 copy-start.9
  187.3 4.0 %copy-start.6 = (f32[256,4,128]{0,2,1:T(8,128)S(1)}, f32[256,4,128]{0,2,1:T(8,128)}, u32[]{:S(2)}) copy-start(f32[256,4,128]{0,2,1:T(8,128)} %get-tuple-element.522) | copy-start | bytes 1572868 | tf_op jit(solution)/shard_map/while
  191.3 4.5 %copy-start.8 = (f32[256,4,128]{0,2,1:T(8,128)S(1)}, f32[256,4,128]{0,2,1:T(8,128)}, u32[]{:S(2)}) copy-start(f32[256,4,128]{0,2,1:T(8,128)} %get-tuple-element.523) | copy-start | bytes 1572868 | tf_op jit(solution)/shard_map/while
  195.8 3.3 %copy-start.7 = (f32[256,4,128]{0,2,1:T(8,128)}, f32[256,4,128]{0,2,1:T(8,128)S(1)}, u32[]{:S(2)}) copy-start(f32[256,4,128]{0,2,1:T(8,128)S(1)} %fusion.120) | copy-start | bytes 1572868 | tf_op jit(solution)/shard_map/while
  199.1 0.8 copy-start.9
Sparse Core Ops, SparseCore 0:
  10.2 38.0 all-gather.4
  49.9 27.1 all-gather.6
  78.6 46.3 all-gather.8
  126.5 44.6 all-gather.10
where the time goes:
time: 211 us; the launch traced here: 210 us
  waiting for transfers between devices  93.5 us (44%)
  matrix products  43.7 us (21%)
  blocking collectives  26.7 us (13%)
  local copies, waits for them, and re-layouts  19.2 us (9%)
  between operations  14 us (7%)
  other arithmetic  7.86 us (4%)
  starting transfers between devices  5.26 us (2%)
    all_gather x1, waiting for transfers between devices, body(): lax.all_gather(cotan_slots.reshape(slot_rows, model_width), 'tm', axis=0,...  43.1 us
    all_gather x1, waiting for transfers between devices, body(): lax.all_gather(value_rows, 'tm', axis=0, tiled=True)  22.5 us
    all_gather x1, blocking collectives, body(): lax.all_gather(log_norm, 'tm', axis=0, tiled=True)  13.4 us
    all_gather x1, blocking collectives, body(): lax.all_gather(deltas, 'tm', axis=0, tiled=True)  13.3 us
    ppermute x1, waiting for transfers between devices, extended_2(): before = lax.ppermute(last, axis, up)  10.1 us
    ppermute x1, waiting for transfers between devices, extended_2(): after = lax.ppermute(first, axis, down)  9.6 us
    dot_general x2, matrix products, owner_work(): jnp.einsum('qhk,qhd->khd', score_grad, query_three, preferred_element_typ...  9.05 us
    unnamed x27, local copies, waits for them, and re-layouts  8.95 us
  transfers between devices with their start and end apart: 6, of which 5 were waited for; matrix products, arithmetic and copies ran while one was open for 17% of the time, Pallas kernels for 0%

commit v1 on v0

--- a/solution.py
+++ b/solution.py
@@ -1,8 +1,11 @@
+import functools
 import math
 
 import jax
 import jax.numpy as jnp
 from jax import lax
+from jax.experimental import pallas as pl
+from jax.experimental.pallas import tpu as pltpu
 from jax.sharding import PartitionSpec as P
 
 HD = 128
@@ -253,6 +256,299 @@
     return (attended.reshape(slot_rows, model_width), query_grad, key_grad, value_grad)
 
 
+def head_kernel(
+    shards,
+    rows,
+    act_ref,
+    cnt_ref,
+    mask_ref,
+    q_hbm,
+    k_hbm,
+    v_hbm,
+    g_hbm,
+    att_hbm,
+    dq_hbm,
+    dk_hbm,
+    dv_hbm,
+    held,
+    scores,
+    weights,
+    grads,
+    key_sum,
+    value_sum,
+    stage,
+    stage_kv,
+    in_send,
+    in_recv,
+    out_send,
+    out_recv,
+    kv_send,
+    kv_recv,
+    in_local,
+    out_local,
+    kv_local,
+):
+    me = lax.axis_index("tm")
+    total = shards * rows
+    blocks = total // BLK
+    scaling = 1.0 / math.sqrt(HD)
+    sources = (k_hbm, v_hbm, q_hbm, g_hbm)
+    outs = (att_hbm, dq_hbm)
+    kv_outs = (dk_hbm, dv_hbm)
+
+    def columns(index):
+        return pl.ds(pl.multiple_of(index * HD, HD), HD)
+
+    def shard_rows(index):
+        return pl.ds(pl.multiple_of(index * rows, rows), rows)
+
+    def incoming(array, source, target):
+        return pltpu.make_async_remote_copy(
+            src_ref=sources[array].at[:, columns(target)],
+            dst_ref=held.at[array, shard_rows(source), :],
+            send_sem=in_send.at[array, target],
+            recv_sem=in_recv.at[array, source],
+            device_id={"tm": target},
+            device_id_type=pl.DeviceIdType.MESH,
+        )
+
+    def own_incoming(array):
+        return pltpu.make_async_copy(
+            sources[array].at[:, columns(me)],
+            held.at[array, shard_rows(me), :],
+            in_local.at[array],
+        )
+
+    pieces = (
+        (shards - 1, 0, (rows // BLK + 1) * BLK, BLK),
+        (0, BLK, BLK, rows),
+        (1, BLK + rows, 0, BLK),
+    )
+
+    def outgoing(array, piece, chunk, target, source):
+        _, low, slot_low, size = pieces[piece]
+        return pltpu.make_async_remote_copy(
+            src_ref=stage.at[array, chunk, pl.ds(low, size), :],
+            dst_ref=outs[array].at[pl.ds(slot_low, size), columns(source)],
+            send_sem=out_send.at[array, piece, chunk],
+            recv_sem=out_recv.at[array, piece, source],
+            device_id={"tm": target},
+            device_id_type=pl.DeviceIdType.MESH,
+        )
+
+    def own_outgoing(array, piece, chunk):
+        _, low, slot_low, size = pieces[piece]
+        return pltpu.make_async_copy(
+            stage.at[array, chunk, pl.ds(low, size), :],
+            outs[array].at[pl.ds(slot_low, size), columns(me)],
+            out_local.at[array, piece],
+        )
+
+    def send_pieces(array, chunk):
+        for piece in range(3):
+            target = lax.rem(chunk + pieces[piece][0], shards)
+
+            @pl.when(target == me)
+            def _():
+                own_outgoing(array, piece, chunk).start()
+
+            @pl.when(target != me)
+            def _():
+                outgoing(array, piece, chunk, target, me).start()
+
+    def kv_outgoing(array, source, target):
+        return pltpu.make_async_remote_copy(
+            src_ref=stage_kv.at[array, shard_rows(target), :],
+            dst_ref=kv_outs[array].at[:, columns(source)],
+            send_sem=kv_send.at[array, target],
+            recv_sem=kv_recv.at[array, source],
+            device_id={"tm": target},
+            device_id_type=pl.DeviceIdType.MESH,
+        )
+
+    def kv_own(array):
+        return pltpu.make_async_copy(
+            stage_kv.at[array, shard_rows(me), :],
+            kv_outs[array].at[:, columns(me)],
+            kv_local.at[array],
+        )
+
+    barrier = pltpu.get_barrier_semaphore()
+    for step in range(1, shards):
+        pl.semaphore_signal(
+            barrier,
+            inc=1,
+            device_id={"tm": lax.rem(me + step, shards)},
+            device_id_type=pl.DeviceIdType.MESH,
+        )
+    for array in range(4):
+        own_incoming(array).start()
+    pl.semaphore_wait(barrier, shards - 1)
+    for array in range(4):
+        for step in range(1, shards):
+            incoming(array, me, lax.rem(me + step, shards)).start()
+
+    key_sum[...] = jnp.zeros_like(key_sum)
+    value_sum[...] = jnp.zeros_like(value_sum)
+    for array in range(4):
+        own_incoming(array).wait()
+    for array in range(2):
+        for step in range(1, shards):
+            source = lax.rem(me + step, shards)
+            incoming(array, source, me).wait_recv()
+
+    lane_block = lax.broadcasted_iota(jnp.int32, (1, rows), 1) // BLK
+
+    def one_chunk(turn, carry):
+        chunk = lax.rem(me + turn, shards)
+
+        @pl.when(turn > 0)
+        def _():
+            incoming(2, chunk, me).wait_recv()
+            incoming(3, chunk, me).wait_recv()
+
+        own = shard_rows(chunk)
+        query = held[2, own, :]
+        cotan = held[3, own, :]
+        peak = jnp.full((1, rows), very_low, jnp.float32)
+        for b in range(blocks):
+            part = pl.ds(b * BLK, BLK)
+            bias = jnp.full((1, rows), very_low, jnp.float32)
+            for j in range(rows // BLK):
+                a = chunk * (rows // BLK) + j
+                seen = act_ref[b] * act_ref[a] * mask_ref[a, b]
+                level = jnp.where(seen > 0, 0.0, very_low)
+                bias = jnp.where(lane_block == j, level, bias)
+            tile = lax.dot_general(
+                held[0, part, :], query, (((1,), (1,)), ((), ())), preferred_element_type=jnp.float32
+            )
+            tile = tile * scaling + bias
+            scores[part, :] = tile
+            peak = jnp.maximum(peak, jnp.max(tile, axis=0, keepdims=True))
+        peak = jnp.maximum(peak, -1e20)
+        mass = jnp.zeros((1, rows), jnp.float32)
+        for b in range(blocks):
+            part = pl.ds(b * BLK, BLK)
+            tile = jnp.exp(scores[part, :] - peak)
+            scores[part, :] = tile
+            weights[part, :] = tile.astype(jnp.bfloat16)
+            mass = mass + jnp.sum(tile, axis=0, keepdims=True)
+        inverse = 1.0 / jnp.where(mass > 0.0, mass, 1.0)
+        att_t = lax.dot_general(
+            held[1], weights[...], (((0,), (0,)), ((), ())), preferred_element_type=jnp.float32
+        )
+        att_t = (att_t * inverse).astype(jnp.bfloat16).astype(jnp.float32)
+        delta = jnp.sum(jnp.transpose(cotan.astype(jnp.float32)) * att_t, axis=0, keepdims=True)
+        last = rows // BLK - 1
+        to_left = cnt_ref[chunk, 0] > 0
+        to_right = cnt_ref[chunk, 1] > 0
+
+        def stage_slots(array, result):
+            result = result.astype(jnp.bfloat16)
+            first, final = result[:BLK], result[last * BLK :]
+            zero = jnp.zeros_like(first)
+            stage[array, chunk, pl.ds(0, BLK), :] = jnp.where(to_left, first, zero)
+            stage[array, chunk, pl.ds(BLK, BLK), :] = jnp.where(to_left, zero, first)
+            stage[array, chunk, pl.ds(rows, BLK), :] = jnp.where(to_right, zero, final)
+            stage[array, chunk, pl.ds(rows + BLK, BLK), :] = jnp.where(to_right, final, zero)
+
+        stage_slots(0, jnp.transpose(att_t))
+        send_pieces(0, chunk)
+        for b in range(blocks):
+            part = pl.ds(b * BLK, BLK)
+            tile = lax.dot_general(
+                held[1, part, :], cotan, (((1,), (1,)), ((), ())), preferred_element_type=jnp.float32
+            )
+            probs = scores[part, :] * inverse
+            grad = (probs * (tile - delta)).astype(jnp.bfloat16)
+            grads[part, :] = grad
+            key_sum[part, :] += jnp.dot(grad, query, preferred_element_type=jnp.float32)
+            value_sum[part, :] += jnp.dot(
+                probs.astype(jnp.bfloat16), cotan, preferred_element_type=jnp.float32
+            )
+        dq_t = lax.dot_general(
+            held[0], grads[...], (((0,), (0,)), ((), ())), preferred_element_type=jnp.float32
+        )
+        stage_slots(1, jnp.transpose(dq_t * scaling))
+        send_pieces(1, chunk)
+        return carry
+
+    lax.fori_loop(0, shards, one_chunk, 0)
+    stage_kv[0] = (key_sum[...] * scaling).astype(jnp.bfloat16)
+    stage_kv[1] = value_sum[...].astype(jnp.bfloat16)
+    for array in range(2):
+        for step in range(1, shards):
+            kv_outgoing(array, me, lax.rem(me + step, shards)).start()
+        kv_own(array).start()
+
+    for step in range(1, shards):
+        peer = lax.rem(me + step, shards)
+        for array in range(4):
+            incoming(array, me, peer).wait_send()
+        for array in range(2):
+            kv_outgoing(array, me, peer).wait_send()
+            kv_outgoing(array, peer, me).wait_recv()
+            for piece in range(3):
+                outgoing(array, piece, 0, me, peer).wait_recv()
+                target_chunk = lax.rem(peer + shards - pieces[piece][0], shards)
+                outgoing(array, piece, target_chunk, peer, me).wait_send()
+    for array in range(2):
+        kv_own(array).wait()
+        for piece in range(3):
+            own_outgoing(array, piece, 0).wait()
+
+
+def exchanged_heads(queries, key_rows, value_rows, cotangent, block_active, send_counts, block_mask):
+    shards = lax.axis_size("tm")
+    rows, width = queries.shape
+    total = shards * rows
+    slot_rows = rows + 2 * CAP * BLK
+    anywhere = pl.BlockSpec(memory_space=pl.ANY)
+    scalars = pl.BlockSpec(memory_space=pltpu.SMEM)
+    return pl.pallas_call(
+        functools.partial(head_kernel, shards, rows),
+        out_shape=(
+            jax.ShapeDtypeStruct((slot_rows, width), jnp.bfloat16),
+            jax.ShapeDtypeStruct((slot_rows, width), jnp.bfloat16),
+            jax.ShapeDtypeStruct((rows, width), jnp.bfloat16),
+            jax.ShapeDtypeStruct((rows, width), jnp.bfloat16),
+        ),
+        in_specs=[scalars] * 3 + [anywhere] * 4,
+        out_specs=(anywhere,) * 4,
+        scratch_shapes=[
+            pltpu.VMEM((4, total, HD), jnp.bfloat16),
+            pltpu.VMEM((total, rows), jnp.float32),
+            pltpu.VMEM((total, rows), jnp.bfloat16),
+            pltpu.VMEM((total, rows), jnp.bfloat16),
+            pltpu.VMEM((total, HD), jnp.float32),
+            pltpu.VMEM((total, HD), jnp.float32),
+            pltpu.VMEM((2, shards, slot_rows, HD), jnp.bfloat16),
+            pltpu.VMEM((2, total, HD), jnp.bfloat16),
+            pltpu.SemaphoreType.DMA((4, shards)),
+            pltpu.SemaphoreType.DMA((4, shards)),
+            pltpu.SemaphoreType.DMA((2, 3, shards)),
+            pltpu.SemaphoreType.DMA((2, 3, shards)),
+            pltpu.SemaphoreType.DMA((2, shards)),
+            pltpu.SemaphoreType.DMA((2, shards)),
+            pltpu.SemaphoreType.DMA((4,)),
+            pltpu.SemaphoreType.DMA((2, 3)),
+            pltpu.SemaphoreType.DMA((2,)),
+        ],
+        compiler_params=pltpu.CompilerParams(
+            collective_id=0, has_side_effects=True, vmem_limit_bytes=40 * 1024 * 1024
+        ),
+    )(block_active, send_counts, block_mask, queries, key_rows, value_rows, cotangent)
+
+
+def routed(queries, key_rows, value_rows, cotangent, block_active, send_counts, block_mask):
+    shards = lax.axis_size("tm")
+    rows, width = queries.shape
+    args = (queries, key_rows, value_rows, cotangent, block_active, send_counts, block_mask)
+    if shards > 1 and width == shards * HD and rows == 2 * BLK:
+        return exchanged_heads(*args)
+    return body(*args)
+
+
 def solution(mesh):
     in_specs = (
         P(("groups", "tm"), ("head", "mp")),
@@ -269,4 +565,5 @@
         P(("groups", "tm"), ("head", "mp")),
         P(("groups", "tm"), ("head", "mp")),
     )
-    return jax.shard_map(body, mesh=mesh, in_specs=in_specs, out_specs=out_specs, check_vma=False)
+    return jax.shard_map(
+        routed, mesh=mesh, in_specs=in_specs, out_specs=out_specs, check_vma=False)

time: 211 us -> 71.8 us (0.34)
  waiting for transfers between devices: 93.5 us -> 0 us
  Pallas kernels: 0 us -> 62.5 us
  matrix products: 43.7 us -> 0 us
  blocking collectives: 26.7 us -> 0 us
  between operations: 14 us -> 0.65 us
  local copies, waits for them, and re-layouts: 19.2 us -> 8.25 us
  other arithmetic: 7.86 us -> 0 us
  starting transfers between devices: 5.26 us -> 0 us
    all_gather x4 -> x0, waiting for transfers between devices: 73 us -> none  [the longest x1 43.1 us: body(): lax.all_gather(cotan_slots.reshape(slot_rows, model_width), 'tm', axis=0,...]
    pallas_call x0 -> x1, Pallas kernels: none -> 62.5 us  [exchanged_heads(): pl.pallas_call(functools.partial(head_kernel, shards, rows), out_shape=(j...]
    dot_general x14 -> x0, matrix products: 43.7 us -> none  [the longest x2 9.05 us: owner_work(): jnp.einsum('qhk,qhd->khd', score_grad, query_three, preferred_element_typ...]
    all_gather x2 -> x0, blocking collectives: 26.7 us -> none  [the longest x1 13.4 us: body(): lax.all_gather(log_norm, 'tm', axis=0, tiled=True)]
    ppermute x2 -> x0, waiting for transfers between devices: 19.7 us -> none  [the longest x1 10.1 us: extended_2(): before = lax.ppermute(last, axis, up)]
    reduce_sum x2 -> x0, other arithmetic: 5.4 us -> none  [the longest x1 5.31 us: forward(): masses = masses * shrink + jnp.sum(weights, axis=2)]
    ppermute x2 -> x0, starting transfers between devices: 5.1 us -> none  [the longest x1 5.1 us: extended_2(): after = lax.ppermute(first, axis, down)]
    dynamic_slice x4 -> x0, local copies, waits for them, and re-layouts: 3.43 us -> none  [the longest x2 3.42 us: one_turn(): lax.dynamic_slice_in_dim(member, turn_index * step_rows, step_rows, 0)]
  transfers between devices with their start and end apart: 6 -> 0, of which waited for: 5 -> 0; matrix products, arithmetic and copies ran while one was open for 17% -> 0% of each run, Pallas kernels for 0% -> 0%
where the time goes in v1:
time: 71.8 us; the launch traced here: 71.4 us
  Pallas kernels  62.5 us (87%)
  local copies, waits for them, and re-layouts  8.25 us (11%)
    pallas_call x1, Pallas kernels, exchanged_heads(): pl.pallas_call(functools.partial(head_kernel, shards, rows), out_shape=(j...  62.5 us
    unnamed x17, local copies, waits for them, and re-layouts  8.25 us

profile of v1, /device:TPU:0, one launch (start us, length us, event | category | flops | bytes accessed | tf_op | source)
XLA Modules:
  0.0 71.4 jit_solution(3621106243646574827)
XLA Ops:
  0.6 0.0 copy-start.5
  0.6 0.8 %copy.11.cnt_ref = s32[4,2]{1,0:T(4,128)S(1)} copy(s32[4,2]{0,1:T(2,128)} %param.12) | data formatting | bytes 64 | tf_op args[5]
  1.4 0.0 copy-done.5
  1.4 0.0 copy-start
  1.4 0.9 %copy-done = bf16[256,512]{1,0:T(8,128)(2,1)S(1)} copy-done((bf16[256,512]{1,0:T(8,128)(2,1)S(1)}, bf16[256,512]{1,0:T(8,128)(2,1)}, u32[]{:S(2)}) %copy-start) | copy-done | bytes 262168
  2.4 0.0 copy-start.1
  2.4 0.9 %copy-done.1 = bf16[256,512]{1,0:T(8,128)(2,1)S(1)} copy-done((bf16[256,512]{1,0:T(8,128)(2,1)S(1)}, bf16[256,512]{1,0:T(8,128)(2,1)}, u32[]{:S(2)}) %copy-start.1) | copy-done | bytes 262168
  3.3 0.0 copy-start.2
  3.3 0.9 %copy-done.2 = bf16[256,512]{1,0:T(8,128)(2,1)S(1)} copy-done((bf16[256,512]{1,0:T(8,128)(2,1)S(1)}, bf16[256,512]{1,0:T(8,128)(2,1)}, u32[]{:S(2)}) %copy-start.2) | copy-done | bytes 262168
  4.3 0.0 copy-start.3
  4.3 0.9 %copy-done.3 = bf16[256,512]{1,0:T(8,128)(2,1)S(1)} copy-done((bf16[256,512]{1,0:T(8,128)(2,1)S(1)}, bf16[256,512]{1,0:T(8,128)(2,1)}, u32[]{:S(2)}) %copy-start.3) | copy-done | bytes 262168
  5.2 0.0 copy-start.4
  5.2 0.7 copy-done.4
  5.9 62.5 %shard_map.102 = (bf16[512,512]{1,0:T(8,128)(2,1)S(1)}, bf16[512,512]{1,0:T(8,128)(2,1)S(1)}, bf16[256,512]{1,0:T(8,128)(2,1)S(1)}, bf16[256,512]{1,0:T(8,128)(2,1)S(1)}) custom-call(s32[8]{0:T(128)S(1)} %copy-done.5, s32[4,2]{1,0:T(4,128)S(1)} %copy.11.cnt_ref, s32[8,8]{1,0:T(8,128)S(1)} %copy-done.4, bf16[256,512]{1,0:T(8,128)(2,1)S(1)} %copy-done, ...), custom_call_target="tpu_custom_call" | custom-call | tf_op jit(solution)/shard_map/pallas_call | solution.py:508
  68.4 0.8 %copy.16 = bf16[512,512]{1,0:T(8,128)(2,1)} copy(bf16[512,512]{1,0:T(8,128)(2,1)S(1)} %get-tuple-element.8) | data formatting | bytes 1048576
  69.2 0.8 %copy.17 = bf16[512,512]{1,0:T(8,128)(2,1)} copy(bf16[512,512]{1,0:T(8,128)(2,1)S(1)} %get-tuple-element.9) | data formatting | bytes 1048576
  70.0 0.7 copy.18
  70.7 0.7 copy.19
Async XLA Ops:
  0.6 0.8 %copy-start.5 = (s32[8]{0:T(128)S(1)}, s32[8]{0:T(128)}, u32[]{:S(2)}) copy-start(s32[8]{0:T(128)} %act_ref.1) | copy-start | bytes 100
  1.4 1.0 %copy-start = (bf16[256,512]{1,0:T(8,128)(2,1)S(1)}, bf16[256,512]{1,0:T(8,128)(2,1)}, u32[]{:S(2)}) copy-start(bf16[256,512]{1,0:T(8,128)(2,1)} %q_hbm.1) | copy-start | bytes 786436
  2.4 0.9 %copy-start.1 = (bf16[256,512]{1,0:T(8,128)(2,1)S(1)}, bf16[256,512]{1,0:T(8,128)(2,1)}, u32[]{:S(2)}) copy-start(bf16[256,512]{1,0:T(8,128)(2,1)} %k_hbm.1) | copy-start | bytes 786436
  3.3 0.9 %copy-start.2 = (bf16[256,512]{1,0:T(8,128)(2,1)S(1)}, bf16[256,512]{1,0:T(8,128)(2,1)}, u32[]{:S(2)}) copy-start(bf16[256,512]{1,0:T(8,128)(2,1)} %v_hbm.1) | copy-start | bytes 786436
  4.3 0.9 %copy-start.3 = (bf16[256,512]{1,0:T(8,128)(2,1)S(1)}, bf16[256,512]{1,0:T(8,128)(2,1)}, u32[]{:S(2)}) copy-start(bf16[256,512]{1,0:T(8,128)(2,1)} %g_hbm.1) | copy-start | bytes 786436
  5.2 0.7 copy-start.4

commit v2 on v1

--- a/solution.py
+++ b/solution.py
@@ -400,9 +400,11 @@
     lane_block = lax.broadcasted_iota(jnp.int32, (1, rows), 1) // BLK
 
     def one_chunk(turn, carry):
-        chunk = lax.rem(me + turn, shards)
-
-        @pl.when(turn > 0)
+        pair = turn // 2
+        side = (turn - 2 * pair) * (1 - 2 * lax.rem(me, 2))
+        chunk = lax.rem(me + side + shards // 2 + 2 * pair + shards, shards)
+
+        @pl.when(chunk != me)
         def _():
             incoming(2, chunk, me).wait_recv()
             incoming(3, chunk, me).wait_recv()
@@ -513,7 +515,7 @@
             jax.ShapeDtypeStruct((rows, width), jnp.bfloat16),
             jax.ShapeDtypeStruct((rows, width), jnp.bfloat16),
         ),
-        in_specs=[scalars] * 3 + [anywhere] * 4,
+        in_specs=[scalars] * 3 + [pl.BlockSpec(memory_space=pltpu.HBM)] * 4,
         out_specs=(anywhere,) * 4,
         scratch_shapes=[
             pltpu.VMEM((4, total, HD), jnp.bfloat16),
@@ -544,7 +546,7 @@
     shards = lax.axis_size("tm")
     rows, width = queries.shape
     args = (queries, key_rows, value_rows, cotangent, block_active, send_counts, block_mask)
-    if shards > 1 and width == shards * HD and rows == 2 * BLK:
+    if shards % 2 == 0 and width == shards * HD and rows == 2 * BLK:
         return exchanged_heads(*args)
     return body(*args)
 

time: 71.8 us -> 71.6 us (level)
  no operation moved by 1% of the time
where the time goes in v2:
time: 71.6 us; the launch traced here: 71.4 us
  Pallas kernels  62.4 us (87%)
  local copies, waits for them, and re-layouts  8.25 us (12%)
    pallas_call x1, Pallas kernels, exchanged_heads(): pl.pallas_call(functools.partial(head_kernel, shards, rows), out_shape=(j...  62.4 us
    unnamed x17, local copies, waits for them, and re-layouts  8.25 us

profile of v2, /device:TPU:0, one launch (start us, length us, event | category | flops | bytes accessed | tf_op | source)
XLA Modules:
  0.0 71.4 jit_solution(14522268322783930437)
XLA Ops:
  0.6 0.0 copy-start.5
  0.6 0.8 %copy.11.cnt_ref = s32[4,2]{1,0:T(4,128)S(1)} copy(s32[4,2]{0,1:T(2,128)} %param.12) | data formatting | bytes 64 | tf_op args[5]
  1.4 0.0 copy-done.5
  1.4 0.0 copy-start
  1.4 0.9 %copy-done = bf16[256,512]{1,0:T(8,128)(2,1)S(1)} copy-done((bf16[256,512]{1,0:T(8,128)(2,1)S(1)}, bf16[256,512]{1,0:T(8,128)(2,1)}, u32[]{:S(2)}) %copy-start) | copy-done | bytes 262168
  2.4 0.0 copy-start.1
  2.4 0.9 %copy-done.1 = bf16[256,512]{1,0:T(8,128)(2,1)S(1)} copy-done((bf16[256,512]{1,0:T(8,128)(2,1)S(1)}, bf16[256,512]{1,0:T(8,128)(2,1)}, u32[]{:S(2)}) %copy-start.1) | copy-done | bytes 262168
  3.3 0.0 copy-start.2
  3.3 0.9 %copy-done.2 = bf16[256,512]{1,0:T(8,128)(2,1)S(1)} copy-done((bf16[256,512]{1,0:T(8,128)(2,1)S(1)}, bf16[256,512]{1,0:T(8,128)(2,1)}, u32[]{:S(2)}) %copy-start.2) | copy-done | bytes 262168
  4.3 0.0 copy-start.3
  4.3 0.9 %copy-done.3 = bf16[256,512]{1,0:T(8,128)(2,1)S(1)} copy-done((bf16[256,512]{1,0:T(8,128)(2,1)S(1)}, bf16[256,512]{1,0:T(8,128)(2,1)}, u32[]{:S(2)}) %copy-start.3) | copy-done | bytes 262168
  5.2 0.0 copy-start.4
  5.2 0.7 copy-done.4
  5.9 62.4 %shard_map.102 = (bf16[512,512]{1,0:T(8,128)(2,1)S(1)}, bf16[512,512]{1,0:T(8,128)(2,1)S(1)}, bf16[256,512]{1,0:T(8,128)(2,1)S(1)}, bf16[256,512]{1,0:T(8,128)(2,1)S(1)}) custom-call(s32[8]{0:T(128)S(1)} %copy-done.5, s32[4,2]{1,0:T(4,128)S(1)} %copy.11.cnt_ref, s32[8,8]{1,0:T(8,128)S(1)} %copy-done.4, bf16[256,512]{1,0:T(8,128)(2,1)S(1)} %copy-done, ...), custom_call_target="tpu_custom_call" | custom-call | tf_op jit(solution)/shard_map/pallas_call | solution.py:510
  68.4 0.8 %copy.16 = bf16[512,512]{1,0:T(8,128)(2,1)} copy(bf16[512,512]{1,0:T(8,128)(2,1)S(1)} %get-tuple-element.8) | data formatting | bytes 1048576
  69.2 0.8 %copy.17 = bf16[512,512]{1,0:T(8,128)(2,1)} copy(bf16[512,512]{1,0:T(8,128)(2,1)S(1)} %get-tuple-element.9) | data formatting | bytes 1048576
  69.9 0.7 copy.18
  70.6 0.7 copy.19
Async XLA Ops:
  0.6 0.8 %copy-start.5 = (s32[8]{0:T(128)S(1)}, s32[8]{0:T(128)}, u32[]{:S(2)}) copy-start(s32[8]{0:T(128)} %act_ref.1) | copy-start | bytes 100
  1.4 1.0 %copy-start = (bf16[256,512]{1,0:T(8,128)(2,1)S(1)}, bf16[256,512]{1,0:T(8,128)(2,1)}, u32[]{:S(2)}) copy-start(bf16[256,512]{1,0:T(8,128)(2,1)} %q_hbm.1) | copy-start | bytes 786436
  2.4 0.9 %copy-start.1 = (bf16[256,512]{1,0:T(8,128)(2,1)S(1)}, bf16[256,512]{1,0:T(8,128)(2,1)}, u32[]{:S(2)}) copy-start(bf16[256,512]{1,0:T(8,128)(2,1)} %k_hbm.1) | copy-start | bytes 786436
  3.3 0.9 %copy-start.2 = (bf16[256,512]{1,0:T(8,128)(2,1)S(1)}, bf16[256,512]{1,0:T(8,128)(2,1)}, u32[]{:S(2)}) copy-start(bf16[256,512]{1,0:T(8,128)(2,1)} %v_hbm.1) | copy-start | bytes 786436
  4.3 0.9 %copy-start.3 = (bf16[256,512]{1,0:T(8,128)(2,1)S(1)}, bf16[256,512]{1,0:T(8,128)(2,1)}, u32[]{:S(2)}) copy-start(bf16[256,512]{1,0:T(8,128)(2,1)} %g_hbm.1) | copy-start | bytes 786436
  5.2 0.7 copy-start.4

commit v3 on v2

--- a/solution.py
+++ b/solution.py
@@ -287,8 +287,20 @@
     in_local,
     out_local,
     kv_local,
+    relay_in,
+    relay_own,
+    relay_on,
+    relay_recv,
+    on_send,
+    on_recv,
+    relay_local,
 ):
     me = lax.axis_index("tm")
+    half = me // 2
+    up = lax.rem(me, 2)
+    near = 2 - half
+    neighbour = me + 1 - 2 * up
+    is_near = me == 1 + half
     total = shards * rows
     blocks = total // BLK
     scaling = 1.0 / math.sqrt(HD)
@@ -344,8 +356,73 @@
             out_local.at[array, piece],
         )
 
+    def middle_half(array, chunk, source):
+        low = pl.multiple_of(BLK + lax.rem(chunk, 2) * BLK, BLK)
+        return pltpu.make_async_remote_copy(
+            src_ref=stage.at[array, chunk, pl.ds(low, BLK), :],
+            dst_ref=outs[array].at[pl.ds(low, BLK), columns(source)],
+            send_sem=out_send.at[array, 1, chunk],
+            recv_sem=out_recv.at[array, 1, source],
+            device_id={"tm": chunk},
+            device_id_type=pl.DeviceIdType.MESH,
+        )
+
+    def to_relay(array, odd, chunk, source_place):
+        low = 0 if odd else BLK + rows
+        return pltpu.make_async_remote_copy(
+            src_ref=stage.at[array, chunk, pl.ds(low, BLK), :],
+            dst_ref=relay_in.at[array, source_place, pl.ds(odd * BLK, BLK), :],
+            send_sem=out_send.at[array, 0 if odd else 2, chunk],
+            recv_sem=relay_recv.at[array, odd, source_place],
+            device_id={"tm": near},
+            device_id_type=pl.DeviceIdType.MESH,
+        )
+
+    def handed_on(array, place, slot_low):
+        source = 2 * (1 - half) + place
+        return pltpu.make_async_remote_copy(
+            src_ref=relay_on.at[array, place],
+            dst_ref=outs[array].at[
+                pl.ds(pl.multiple_of(slot_low, 2 * BLK), 2 * BLK), columns(source)
+            ],
+            send_sem=on_send.at[array, place],
+            recv_sem=on_recv.at[array, place],
+            device_id={"tm": neighbour},
+            device_id_type=pl.DeviceIdType.MESH,
+        )
+
+    def relay_kept(array, place):
+        source = 2 * (1 - half) + place
+        return pltpu.make_async_copy(
+            relay_own.at[array, place],
+            outs[array].at[
+                pl.ds(pl.multiple_of((1 - up) * 2 * BLK, 2 * BLK), 2 * BLK), columns(source)
+            ],
+            relay_local.at[array, place],
+        )
+
     def send_pieces(array, chunk):
-        for piece in range(3):
+        far = chunk // 2 != half
+        odd = lax.rem(chunk, 2) == 1
+
+        @pl.when(jnp.logical_not(far))
+        def _():
+            send_some(array, chunk, (0, 1, 2))
+
+        @pl.when(far & jnp.logical_not(odd))
+        def _():
+            send_some(array, chunk, (0,))
+            middle_half(array, chunk, me).start()
+            to_relay(array, 0, chunk, up).start()
+
+        @pl.when(far & odd)
+        def _():
+            send_some(array, chunk, (2,))
+            middle_half(array, chunk, me).start()
+            to_relay(array, 1, chunk, up).start()
+
+    def send_some(array, chunk, which):
+        for piece in which:
             target = lax.rem(chunk + pieces[piece][0], shards)
 
             @pl.when(target == me)
@@ -445,14 +522,18 @@
         to_left = cnt_ref[chunk, 0] > 0
         to_right = cnt_ref[chunk, 1] > 0
 
+        far = chunk // 2 != half
+        raw_first = to_left | (far & (lax.rem(chunk, 2) == 1))
+        raw_final = to_right | (far & (lax.rem(chunk, 2) == 0))
+
         def stage_slots(array, result):
             result = result.astype(jnp.bfloat16)
             first, final = result[:BLK], result[last * BLK :]
             zero = jnp.zeros_like(first)
-            stage[array, chunk, pl.ds(0, BLK), :] = jnp.where(to_left, first, zero)
+            stage[array, chunk, pl.ds(0, BLK), :] = jnp.where(raw_first, first, zero)
             stage[array, chunk, pl.ds(BLK, BLK), :] = jnp.where(to_left, zero, first)
             stage[array, chunk, pl.ds(rows, BLK), :] = jnp.where(to_right, zero, final)
-            stage[array, chunk, pl.ds(rows + BLK, BLK), :] = jnp.where(to_right, final, zero)
+            stage[array, chunk, pl.ds(rows + BLK, BLK), :] = jnp.where(raw_final, final, zero)
 
         stage_slots(0, jnp.transpose(att_t))
         send_pieces(0, chunk)
@@ -483,6 +564,34 @@
             kv_outgoing(array, me, lax.rem(me + step, shards)).start()
         kv_own(array).start()
 
+    @pl.when(is_near)
+    def _():
+        lower = me - up
+        right = cnt_ref[lower, 1]
+        left = cnt_ref[lower + 1, 0]
+        for array in range(2):
+            for place in range(2):
+                to_relay(array, 0, lower, place).wait_recv()
+                to_relay(array, 1, lower + 1, place).wait_recv()
+                for b, keep in ((0, right == up), (1, left == 1 - up)):
+                    part = pl.ds(b * BLK, BLK)
+                    block = relay_in[array, place, part, :]
+                    zero = jnp.zeros_like(block)
+                    relay_own[array, place, part, :] = jnp.where(keep, block, zero)
+                    relay_on[array, place, part, :] = jnp.where(keep, zero, block)
+                handed_on(array, place, up * 2 * BLK).start()
+                relay_kept(array, place).start()
+        for array in range(2):
+            for place in range(2):
+                handed_on(array, place, up * 2 * BLK).wait_send()
+                relay_kept(array, place).wait()
+
+    @pl.when(jnp.logical_not(is_near))
+    def _():
+        for array in range(2):
+            for place in range(2):
+                handed_on(array, place, (1 - up) * 2 * BLK).wait_recv()
+
     for step in range(1, shards):
         peer = lax.rem(me + step, shards)
         for array in range(4):
@@ -490,10 +599,36 @@
         for array in range(2):
             kv_outgoing(array, me, peer).wait_send()
             kv_outgoing(array, peer, me).wait_recv()
-            for piece in range(3):
-                outgoing(array, piece, 0, me, peer).wait_recv()
-                target_chunk = lax.rem(peer + shards - pieces[piece][0], shards)
-                outgoing(array, piece, target_chunk, peer, me).wait_send()
+
+        @pl.when(peer // 2 == half)
+        def _():
+            for array in range(2):
+                for piece in range(3):
+                    outgoing(array, piece, 0, me, peer).wait_recv()
+                outgoing(array, 1, peer, peer, me).wait_send()
+
+        @pl.when(peer // 2 != half)
+        def _():
+            for array in range(2):
+                middle_half(array, me, peer).wait_recv()
+                middle_half(array, peer, me).wait_send()
+
+            @pl.when(up == 0)
+            def _():
+                for array in range(2):
+                    outgoing(array, 2, 0, me, peer).wait_recv()
+
+            @pl.when(up == 1)
+            def _():
+                for array in range(2):
+                    outgoing(array, 0, 0, me, peer).wait_recv()
+
+    for step in range(shards):
+        chunk = lax.rem(me + step, shards)
+        for piece in (0, 2):
+            if (step + pieces[piece][0]) % shards != 0:
+                for array in range(2):
+                    outgoing(array, piece, chunk, near, me).wait_send()
     for array in range(2):
         kv_own(array).wait()
         for piece in range(3):
@@ -535,9 +670,16 @@
             pltpu.SemaphoreType.DMA((4,)),
             pltpu.SemaphoreType.DMA((2, 3)),
             pltpu.SemaphoreType.DMA((2,)),
+            pltpu.VMEM((2, 2, 2 * BLK, HD), jnp.bfloat16),
+            pltpu.VMEM((2, 2, 2 * BLK, HD), jnp.bfloat16),
+            pltpu.VMEM((2, 2, 2 * BLK, HD), jnp.bfloat16),
+            pltpu.SemaphoreType.DMA((2, 2, 2)),
+            pltpu.SemaphoreType.DMA((2, 2)),
+            pltpu.SemaphoreType.DMA((2, 2)),
+            pltpu.SemaphoreType.DMA((2, 2)),
         ],
         compiler_params=pltpu.CompilerParams(
-            collective_id=0, has_side_effects=True, vmem_limit_bytes=40 * 1024 * 1024
+            collective_id=0, has_side_effects=True, vmem_limit_bytes=63 * 1024 * 1024
         ),
     )(block_active, send_counts, block_mask, queries, key_rows, value_rows, cotangent)
 
@@ -546,7 +688,7 @@
     shards = lax.axis_size("tm")
     rows, width = queries.shape
     args = (queries, key_rows, value_rows, cotangent, block_active, send_counts, block_mask)
-    if shards % 2 == 0 and width == shards * HD and rows == 2 * BLK:
+    if shards == 4 and width == shards * HD and rows == 2 * BLK:
         return exchanged_heads(*args)
     return body(*args)
 

time: 71.6 us -> 66.2 us (0.925)
  Pallas kernels: 62.4 us -> 59.2 us
  local copies, waits for them, and re-layouts: 8.25 us -> 6.1 us
    pallas_call x1, Pallas kernels: 62.4 us -> 59.2 us  [exchanged_heads(): pl.pallas_call(functools.partial(head_kernel, shards, rows), out_shape=(j...]
    unnamed x17 -> x11, local copies, waits for them, and re-layouts: 8.25 us -> 6.1 us
where the time goes in v3:
time: 66.2 us; the launch traced here: 66 us
  Pallas kernels  59.2 us (89%)
  local copies, waits for them, and re-layouts  6.1 us (9%)
    pallas_call x1, Pallas kernels, exchanged_heads(): pl.pallas_call(functools.partial(head_kernel, shards, rows), out_shape=(j...  59.2 us
    unnamed x11, local copies, waits for them, and re-layouts  6.1 us

profile of v3, /device:TPU:0, one launch (start us, length us, event | category | flops | bytes accessed | tf_op | source)
XLA Modules:
  0.0 66.0 jit_solution(14732626247557807709)
XLA Ops:
  0.6 1.3 %copy.11.cnt_ref = s32[4,2]{1,0:T(4,128)} copy(s32[4,2]{0,1:T(2,128)} %param.12) | data formatting | bytes 64 | tf_op args[5]
  2.0 59.2 %shard_map.102 = (bf16[512,512]{1,0:T(8,128)(2,1)}, bf16[512,512]{1,0:T(8,128)(2,1)}, bf16[256,512]{1,0:T(8,128)(2,1)}, bf16[256,512]{1,0:T(8,128)(2,1)}) custom-call(s32[8]{0:T(128)} %act_ref.1, s32[4,2]{1,0:T(4,128)} %copy.11.cnt_ref, s32[8,8]{1,0:T(8,128)} %mask_ref.1, bf16[256,512]{1,0:T(8,128)(2,1)} %q_hbm.1, bf16[256,512]{1,0:T(8,128)(2,1)} %k_hbm.1, ...), custom_call_target="tpu_custom_call" | custom-call | tf_op jit(solution)/shard_map/pallas_call | solution.py:645
  61.2 0.0 copy-start
  61.2 1.9 %copy.16 = bf16[512,512]{1,0:T(8,128)(2,1)} copy(bf16[512,512]{1,0:T(8,128)(2,1)} %get-tuple-element.8) | data formatting | bytes 1048576
  63.1 0.0 copy-done
  63.1 0.0 copy-start.2
  63.1 0.8 %copy.17 = bf16[512,512]{1,0:T(8,128)(2,1)} copy(bf16[512,512]{1,0:T(8,128)(2,1)S(1)} %copy-done) | data formatting | bytes 1048576
  63.9 0.3 copy-done.2
  64.2 0.0 copy-start.1
  64.2 0.7 %copy.18 = bf16[256,512]{1,0:T(8,128)(2,1)} copy(bf16[256,512]{1,0:T(8,128)(2,1)S(1)} %copy-done.2) | data formatting | bytes 524288
  64.9 0.3 copy-done.1
  65.3 0.7 %copy.19 = bf16[256,512]{1,0:T(8,128)(2,1)} copy(bf16[256,512]{1,0:T(8,128)(2,1)S(1)} %copy-done.1) | data formatting | bytes 524288
Async XLA Ops:
  61.2 1.9 %copy-start = (bf16[512,512]{1,0:T(8,128)(2,1)S(1)}, bf16[512,512]{1,0:T(8,128)(2,1)}, u32[]{:S(2)}) copy-start(bf16[512,512]{1,0:T(8,128)(2,1)} %get-tuple-element.9) | copy-start | bytes 1572868
  63.1 1.1 %copy-start.2 = (bf16[256,512]{1,0:T(8,128)(2,1)S(1)}, bf16[256,512]{1,0:T(8,128)(2,1)}, u32[]{:S(2)}) copy-start(bf16[256,512]{1,0:T(8,128)(2,1)} %get-tuple-element.10) | copy-start | bytes 786436
  64.2 1.0 %copy-start.1 = (bf16[256,512]{1,0:T(8,128)(2,1)S(1)}, bf16[256,512]{1,0:T(8,128)(2,1)}, u32[]{:S(2)}) copy-start(bf16[256,512]{1,0:T(8,128)(2,1)} %get-tuple-element.11) | copy-start | bytes 786436

commit v4 on v3

--- a/solution.py
+++ b/solution.py
@@ -519,8 +519,8 @@
         att_t = (att_t * inverse).astype(jnp.bfloat16).astype(jnp.float32)
         delta = jnp.sum(jnp.transpose(cotan.astype(jnp.float32)) * att_t, axis=0, keepdims=True)
         last = rows // BLK - 1
-        to_left = cnt_ref[chunk, 0] > 0
-        to_right = cnt_ref[chunk, 1] > 0
+        to_left = cnt_ref[0, chunk] > 0
+        to_right = cnt_ref[1, chunk] > 0
 
         far = chunk // 2 != half
         raw_first = to_left | (far & (lax.rem(chunk, 2) == 1))
@@ -567,8 +567,8 @@
     @pl.when(is_near)
     def _():
         lower = me - up
-        right = cnt_ref[lower, 1]
-        left = cnt_ref[lower + 1, 0]
+        right = cnt_ref[1, lower]
+        left = cnt_ref[0, lower + 1]
         for array in range(2):
             for place in range(2):
                 to_relay(array, 0, lower, place).wait_recv()
@@ -681,7 +681,7 @@
         compiler_params=pltpu.CompilerParams(
             collective_id=0, has_side_effects=True, vmem_limit_bytes=63 * 1024 * 1024
         ),
-    )(block_active, send_counts, block_mask, queries, key_rows, value_rows, cotangent)
+    )(block_active, send_counts.T, block_mask, queries, key_rows, value_rows, cotangent)
 
 
 def routed(queries, key_rows, value_rows, cotangent, block_active, send_counts, block_mask):

time: 66.2 us -> 64.9 us (0.980)
  local copies, waits for them, and re-layouts: 6.1 us -> 4.77 us
    unnamed x11 -> x10, local copies, waits for them, and re-layouts: 6.1 us -> 4.77 us
where the time goes in v4:
time: 64.9 us; the launch traced here: 64.6 us
  Pallas kernels  59.2 us (91%)
  local copies, waits for them, and re-layouts  4.77 us (7%)
  between operations  0.65 us (1%)
    pallas_call x1, Pallas kernels, exchanged_heads(): pl.pallas_call(functools.partial(head_kernel, shards, rows), out_shape=(j...  59.2 us
    unnamed x10, local copies, waits for them, and re-layouts  4.77 us

profile of v4, /device:TPU:0, one launch (start us, length us, event | category | flops | bytes accessed | tf_op | source)
XLA Modules:
  0.0 64.6 jit_solution(3075409363634383555)
XLA Ops:
  0.6 59.2 %shard_map.102 = (bf16[512,512]{1,0:T(8,128)(2,1)}, bf16[512,512]{1,0:T(8,128)(2,1)}, bf16[256,512]{1,0:T(8,128)(2,1)}, bf16[256,512]{1,0:T(8,128)(2,1)}) custom-call(s32[8]{0:T(128)} %act_ref.1, s32[2,4]{1,0:T(2,128)} %bitcast.1, s32[8,8]{1,0:T(8,128)} %mask_ref.1, bf16[256,512]{1,0:T(8,128)(2,1)} %q_hbm.1, bf16[256,512]{1,0:T(8,128)(2,1)} %k_hbm.1, ...), custom_call_target="tpu_custom_call" | custom-call | tf_op jit(solution)/shard_map/pallas_call | solution.py:645
  59.9 0.0 copy-start
  59.9 1.9 %copy.15 = bf16[512,512]{1,0:T(8,128)(2,1)} copy(bf16[512,512]{1,0:T(8,128)(2,1)} %get-tuple-element.8) | data formatting | bytes 1048576
  61.8 0.0 copy-done
  61.8 0.0 copy-start.2
  61.8 0.8 %copy.16 = bf16[512,512]{1,0:T(8,128)(2,1)} copy(bf16[512,512]{1,0:T(8,128)(2,1)S(1)} %copy-done) | data formatting | bytes 1048576
  62.6 0.3 copy-done.2
  62.9 0.0 copy-start.1
  62.9 0.7 %copy.17 = bf16[256,512]{1,0:T(8,128)(2,1)} copy(bf16[256,512]{1,0:T(8,128)(2,1)S(1)} %copy-done.2) | data formatting | bytes 524288
  63.6 0.3 copy-done.1
  63.9 0.7 %copy.18 = bf16[256,512]{1,0:T(8,128)(2,1)} copy(bf16[256,512]{1,0:T(8,128)(2,1)S(1)} %copy-done.1) | data formatting | bytes 524288
Async XLA Ops:
  59.9 1.9 %copy-start = (bf16[512,512]{1,0:T(8,128)(2,1)S(1)}, bf16[512,512]{1,0:T(8,128)(2,1)}, u32[]{:S(2)}) copy-start(bf16[512,512]{1,0:T(8,128)(2,1)} %get-tuple-element.9) | copy-start | bytes 1572868
  61.8 1.1 %copy-start.2 = (bf16[256,512]{1,0:T(8,128)(2,1)S(1)}, bf16[256,512]{1,0:T(8,128)(2,1)}, u32[]{:S(2)}) copy-start(bf16[256,512]{1,0:T(8,128)(2,1)} %get-tuple-element.10) | copy-start | bytes 786436
  62.9 1.0 %copy-start.1 = (bf16[256,512]{1,0:T(8,128)(2,1)S(1)}, bf16[256,512]{1,0:T(8,128)(2,1)}, u32[]{:S(2)}) copy-start(bf16[256,512]{1,0:T(8,128)(2,1)} %get-tuple-element.11) | copy-start | bytes 786436

commit v5 on v4

--- a/solution.py
+++ b/solution.py
@@ -635,6 +635,18 @@
             own_outgoing(array, piece, 0).wait()
 
 
+def hand_out(*refs):
+    count = len(refs) // 2
+    done = refs[-1]
+    copies = [
+        pltpu.make_async_copy(refs[i], refs[count + i], done.at[i]) for i in range(count)
+    ]
+    for copy in copies:
+        copy.start()
+    for copy in copies:
+        copy.wait()
+
+
 def exchanged_heads(queries, key_rows, value_rows, cotangent, block_active, send_counts, block_mask):
     shards = lax.axis_size("tm")
     rows, width = queries.shape
@@ -642,7 +654,7 @@
     slot_rows = rows + 2 * CAP * BLK
     anywhere = pl.BlockSpec(memory_space=pl.ANY)
     scalars = pl.BlockSpec(memory_space=pltpu.SMEM)
-    return pl.pallas_call(
+    results = pl.pallas_call(
         functools.partial(head_kernel, shards, rows),
         out_shape=(
             jax.ShapeDtypeStruct((slot_rows, width), jnp.bfloat16),
@@ -682,6 +694,13 @@
             collective_id=0, has_side_effects=True, vmem_limit_bytes=63 * 1024 * 1024
         ),
     )(block_active, send_counts.T, block_mask, queries, key_rows, value_rows, cotangent)
+    return pl.pallas_call(
+        hand_out,
+        out_shape=tuple(jax.ShapeDtypeStruct(r.shape, r.dtype) for r in results),
+        in_specs=[anywhere] * 4,
+        out_specs=(anywhere,) * 4,
+        scratch_shapes=[pltpu.SemaphoreType.DMA((4,))],
+    )(*results)
 
 
 def routed(queries, key_rows, value_rows, cotangent, block_active, send_counts, block_mask):

time: 64.9 us -> 109 us (1.68)
  Pallas kernels: 59.2 us -> 108 us
  local copies, waits for them, and re-layouts: 4.77 us -> 0 us
    pallas_call x0 -> x1, Pallas kernels: none -> 48.8 us  [exchanged_heads(): pl.pallas_call(hand_out, out_shape=tuple((jax.ShapeDtypeStruct(r.shape, r...]
    unnamed x10 -> x0, local copies, waits for them, and re-layouts: 4.77 us -> none
where the time goes in v5:
time: 109 us
  Pallas kernels  108 us (99%)
    pallas_call x1, Pallas kernels, exchanged_heads(): pl.pallas_call(functools.partial(head_kernel, shards, rows), out_shape=(j...  59.2 us
    pallas_call x1, Pallas kernels, exchanged_heads(): pl.pallas_call(hand_out, out_shape=tuple((jax.ShapeDtypeStruct(r.shape, r...  48.8 us

profile of v5, /device:TPU:0, one launch (start us, length us, event | category | flops | bytes accessed | tf_op | source)
XLA Modules:
  0.0 108.6 jit_solution(13393324295563328507)
XLA Ops:
  0.6 59.2 %shard_map.102 = (bf16[512,512]{1,0:T(8,128)(2,1)}, bf16[512,512]{1,0:T(8,128)(2,1)}, bf16[256,512]{1,0:T(8,128)(2,1)}, bf16[256,512]{1,0:T(8,128)(2,1)}) custom-call(s32[8]{0:T(128)} %act_ref.1, s32[2,4]{1,0:T(2,128)} %bitcast.1, s32[8,8]{1,0:T(8,128)} %mask_ref.1, bf16[256,512]{1,0:T(8,128)(2,1)} %q_hbm.1, bf16[256,512]{1,0:T(8,128)(2,1)} %k_hbm.1, ...), custom_call_target="tpu_custom_call" | custom-call | tf_op jit(solution)/shard_map/pallas_call | solution.py:657
  59.9 48.8 %shard_map.103 = (bf16[512,512]{1,0:T(8,128)(2,1)}, bf16[512,512]{1,0:T(8,128)(2,1)}, bf16[256,512]{1,0:T(8,128)(2,1)}, bf16[256,512]{1,0:T(8,128)(2,1)}) custom-call(bf16[512,512]{1,0:T(8,128)(2,1)} %get-tuple-element.8.refs_0_, bf16[512,512]{1,0:T(8,128)(2,1)} %get-tuple-element.9.refs_1_, bf16[256,512]{1,0:T(8,128)(2,1)} %get-tuple-element.10.refs_2_, ...), custom_call_target="tpu_custom_call" | custom-call | tf_op jit(solution)/shard_map/pallas_call | solution.py:697

commit v6 on v5

--- a/solution.py
+++ b/solution.py
@@ -636,14 +636,17 @@
 
 
 def hand_out(*refs):
-    count = len(refs) // 2
-    done = refs[-1]
-    copies = [
-        pltpu.make_async_copy(refs[i], refs[count + i], done.at[i]) for i in range(count)
-    ]
-    for copy in copies:
+    count = 4
+    sources, targets, held = refs[:count], refs[count : 2 * count], refs[2 * count : 3 * count]
+    arrived, left = refs[3 * count :]
+    inward = [pltpu.make_async_copy(sources[i], held[i], arrived.at[i]) for i in range(count)]
+    outward = [pltpu.make_async_copy(held[i], targets[i], left.at[i]) for i in range(count)]
+    for copy in inward:
         copy.start()
-    for copy in copies:
+    for first, second in zip(inward, outward):
+        first.wait()
+        second.start()
+    for copy in outward:
         copy.wait()
 
 
@@ -699,7 +702,8 @@
         out_shape=tuple(jax.ShapeDtypeStruct(r.shape, r.dtype) for r in results),
         in_specs=[anywhere] * 4,
         out_specs=(anywhere,) * 4,
-        scratch_shapes=[pltpu.SemaphoreType.DMA((4,))],
+        scratch_shapes=[pltpu.VMEM(r.shape, r.dtype) for r in results]
+        + [pltpu.SemaphoreType.DMA((4,)), pltpu.SemaphoreType.DMA((4,))],
     )(*results)
 
 

time: 109 us -> 62.3 us (0.57)
  Pallas kernels: 108 us -> 61.5 us
    pallas_call x1, Pallas kernels: 48.8 us -> 2.25 us  [exchanged_heads(): pl.pallas_call(hand_out, out_shape=tuple((jax.ShapeDtypeStruct(r.shape, r...]
where the time goes in v6:
time: 62.3 us; the launch traced here: 62.1 us
  Pallas kernels  61.5 us (99%)
  between operations  0.64 us (1%)
    pallas_call x1, Pallas kernels, exchanged_heads(): pl.pallas_call(functools.partial(head_kernel, shards, rows), out_shape=(j...  59.2 us
    pallas_call x1, Pallas kernels, exchanged_heads(): pl.pallas_call(hand_out, out_shape=tuple((jax.ShapeDtypeStruct(r.shape, r...  2.25 us

profile of v6, /device:TPU:0, one launch (start us, length us, event | category | flops | bytes accessed | tf_op | source)
XLA Modules:
  0.0 62.1 jit_solution(16934299496832407144)
XLA Ops:
  0.6 59.2 %shard_map.102 = (bf16[512,512]{1,0:T(8,128)(2,1)}, bf16[512,512]{1,0:T(8,128)(2,1)}, bf16[256,512]{1,0:T(8,128)(2,1)}, bf16[256,512]{1,0:T(8,128)(2,1)}) custom-call(s32[8]{0:T(128)} %act_ref.1, s32[2,4]{1,0:T(2,128)} %bitcast.1, s32[8,8]{1,0:T(8,128)} %mask_ref.1, bf16[256,512]{1,0:T(8,128)(2,1)} %q_hbm.1, bf16[256,512]{1,0:T(8,128)(2,1)} %k_hbm.1, ...), custom_call_target="tpu_custom_call" | custom-call | tf_op jit(solution)/shard_map/pallas_call | solution.py:660
  59.9 2.2 %shard_map.103 = (bf16[512,512]{1,0:T(8,128)(2,1)}, bf16[512,512]{1,0:T(8,128)(2,1)}, bf16[256,512]{1,0:T(8,128)(2,1)}, bf16[256,512]{1,0:T(8,128)(2,1)}) custom-call(bf16[512,512]{1,0:T(8,128)(2,1)} %get-tuple-element.8.refs_0_, bf16[512,512]{1,0:T(8,128)(2,1)} %get-tuple-element.9.refs_1_, bf16[256,512]{1,0:T(8,128)(2,1)} %get-tuple-element.10.refs_2_, ...), custom_call_target="tpu_custom_call" | custom-call | tf_op jit(solution)/shard_map/pallas_call | solution.py:700

commit v7 on v6

--- a/solution.py
+++ b/solution.py
@@ -557,13 +557,6 @@
         return carry
 
     lax.fori_loop(0, shards, one_chunk, 0)
-    stage_kv[0] = (key_sum[...] * scaling).astype(jnp.bfloat16)
-    stage_kv[1] = value_sum[...].astype(jnp.bfloat16)
-    for array in range(2):
-        for step in range(1, shards):
-            kv_outgoing(array, me, lax.rem(me + step, shards)).start()
-        kv_own(array).start()
-
     @pl.when(is_near)
     def _():
         lower = me - up
@@ -581,6 +574,16 @@
                     relay_on[array, place, part, :] = jnp.where(keep, zero, block)
                 handed_on(array, place, up * 2 * BLK).start()
                 relay_kept(array, place).start()
+
+    stage_kv[0] = (key_sum[...] * scaling).astype(jnp.bfloat16)
+    stage_kv[1] = value_sum[...].astype(jnp.bfloat16)
+    for array in range(2):
+        for step in range(1, shards):
+            kv_outgoing(array, me, lax.rem(me + step, shards)).start()
+        kv_own(array).start()
+
+    @pl.when(is_near)
+    def _():
         for array in range(2):
             for place in range(2):
                 handed_on(array, place, up * 2 * BLK).wait_send()

time: 62.3 us -> 62.3 us (level)
  no operation moved by 1% of the time
where the time goes in v7:
time: 62.3 us; the launch traced here: 62.1 us
  Pallas kernels  61.4 us (99%)
  between operations  0.64 us (1%)
    pallas_call x1, Pallas kernels, exchanged_heads(): pl.pallas_call(functools.partial(head_kernel, shards, rows), out_shape=(j...  59.2 us
    pallas_call x1, Pallas kernels, exchanged_heads(): pl.pallas_call(hand_out, out_shape=tuple((jax.ShapeDtypeStruct(r.shape, r...  2.25 us

profile of v7, /device:TPU:0, one launch (start us, length us, event | category | flops | bytes accessed | tf_op | source)
XLA Modules:
  0.0 62.1 jit_solution(9613049201474341139)
XLA Ops:
  0.6 59.2 %shard_map.102 = (bf16[512,512]{1,0:T(8,128)(2,1)}, bf16[512,512]{1,0:T(8,128)(2,1)}, bf16[256,512]{1,0:T(8,128)(2,1)}, bf16[256,512]{1,0:T(8,128)(2,1)}) custom-call(s32[8]{0:T(128)} %act_ref.1, s32[2,4]{1,0:T(2,128)} %bitcast.1, s32[8,8]{1,0:T(8,128)} %mask_ref.1, bf16[256,512]{1,0:T(8,128)(2,1)} %q_hbm.1, bf16[256,512]{1,0:T(8,128)(2,1)} %k_hbm.1, ...), custom_call_target="tpu_custom_call" | custom-call | tf_op jit(solution)/shard_map/pallas_call | solution.py:663
  59.8 2.2 %shard_map.103 = (bf16[512,512]{1,0:T(8,128)(2,1)}, bf16[512,512]{1,0:T(8,128)(2,1)}, bf16[256,512]{1,0:T(8,128)(2,1)}, bf16[256,512]{1,0:T(8,128)(2,1)}) custom-call(bf16[512,512]{1,0:T(8,128)(2,1)} %get-tuple-element.8.refs_0_, bf16[512,512]{1,0:T(8,128)(2,1)} %get-tuple-element.9.refs_1_, bf16[256,512]{1,0:T(8,128)(2,1)} %get-tuple-element.10.refs_2_, ...), custom_call_target="tpu_custom_call" | custom-call | tf_op jit(solution)/shard_map/pallas_call | solution.py:703

commit v8 on v7

--- a/solution.py
+++ b/solution.py
@@ -575,10 +575,9 @@
                 handed_on(array, place, up * 2 * BLK).start()
                 relay_kept(array, place).start()
 
-    stage_kv[0] = (key_sum[...] * scaling).astype(jnp.bfloat16)
-    stage_kv[1] = value_sum[...].astype(jnp.bfloat16)
-    for array in range(2):
-        for step in range(1, shards):
+    for array, total_sum, factor in ((0, key_sum, scaling), (1, value_sum, 1.0)):
+        stage_kv[array] = (total_sum[...] * factor).astype(jnp.bfloat16)
+        for step in (2, 1, 3):
             kv_outgoing(array, me, lax.rem(me + step, shards)).start()
         kv_own(array).start()
 

time: 62.3 us -> 62.3 us (level)
  no operation moved by 1% of the time
where the time goes in v8:
time: 62.3 us; the launch traced here: 62.1 us
  Pallas kernels  61.4 us (99%)
  between operations  0.64 us (1%)
    pallas_call x1, Pallas kernels, exchanged_heads(): pl.pallas_call(functools.partial(head_kernel, shards, rows), out_shape=(j...  59.2 us
    pallas_call x1, Pallas kernels, exchanged_heads(): pl.pallas_call(hand_out, out_shape=tuple((jax.ShapeDtypeStruct(r.shape, r...  2.25 us

profile of v8, /device:TPU:0, one launch (start us, length us, event | category | flops | bytes accessed | tf_op | source)
XLA Modules:
  0.0 62.1 jit_solution(4777983032558932918)
XLA Ops:
  0.6 59.2 %shard_map.102 = (bf16[512,512]{1,0:T(8,128)(2,1)}, bf16[512,512]{1,0:T(8,128)(2,1)}, bf16[256,512]{1,0:T(8,128)(2,1)}, bf16[256,512]{1,0:T(8,128)(2,1)}) custom-call(s32[8]{0:T(128)} %act_ref.1, s32[2,4]{1,0:T(2,128)} %bitcast.1, s32[8,8]{1,0:T(8,128)} %mask_ref.1, bf16[256,512]{1,0:T(8,128)(2,1)} %q_hbm.1, bf16[256,512]{1,0:T(8,128)(2,1)} %k_hbm.1, ...), custom_call_target="tpu_custom_call" | custom-call | tf_op jit(solution)/shard_map/pallas_call | solution.py:662
  59.8 2.2 %shard_map.103 = (bf16[512,512]{1,0:T(8,128)(2,1)}, bf16[512,512]{1,0:T(8,128)(2,1)}, bf16[256,512]{1,0:T(8,128)(2,1)}, bf16[256,512]{1,0:T(8,128)(2,1)}) custom-call(bf16[512,512]{1,0:T(8,128)(2,1)} %get-tuple-element.8.refs_0_, bf16[512,512]{1,0:T(8,128)(2,1)} %get-tuple-element.9.refs_1_, bf16[256,512]{1,0:T(8,128)(2,1)} %get-tuple-element.10.refs_2_, ...), custom_call_target="tpu_custom_call" | custom-call | tf_op jit(solution)/shard_map/pallas_call | solution.py:702
